TPU v7x, 32 devices: a whole 2x2x4 slice. The times are simulated.
32 devices in a mesh: proto: 16 (over z, x, core), sample: 2 (over y).
Axes of the slice: x: 2, y: 2, z: 4, core: 2. Of those that a mesh axis runs over, the one named last changes fastest.
Arguments:
- teacher_new: bfloat16 [512, 384], P('sample'), may hold values from -6 to 6
- queue: bfloat16 [1536, 384], P('sample'), may hold values from -6 to 6
- student: bfloat16 [512, 384], P('sample'), may hold values from -6 to 6
- prototypes: bfloat16 [32768, 384], P('proto'), may hold values from -1 to 1
- owners: int32 [512, 1], P('sample'), may hold values from 0 to 1; in each aligned block of 256 rows (0 to 255, 256 to 511, ...) at most 256 rows name the same one
- queue_oldest_slot: int32 [2], P('sample'), may hold values from 0 to 767
Outputs:
- new_queue: bfloat16 [1536, 384], P('sample')
- proto_grad: float32 [32768, 384], P(('proto', 'sample'))
- loss: float32 [], replicated
Inputs may be any that keep to these rules, and one draw needn't show every extreme that they name: `owners`: among the rows of one device (aligned blocks of 256 rows), no owner is named more than 256 times, a bound that some block reaches.
All inputs are finite; a program needn't handle non-finite values.
Results may differ from a plain program's by a relative error of at most 0.0034.
Values may be sent and summed in bfloat16 or wider, within the bound.
A program may use at most 64 MiB of HBM per device.

v0:
```python
import jax
import jax.numpy as jnp
from jax import lax
from jax.sharding import PartitionSpec as P

K_DEV = 2048
NEW_DEV = 256
ITERS = 3
QUEUE_PER_INDEX = 768


teacher_temp = 0.07
student_temp = 0.1
epsilon = 1e-12


def unit_rows(values):
    widened = values.astype(jnp.float32)
    length = jnp.sqrt(jnp.sum(widened * widened, axis=1, keepdims=True) + epsilon)
    return (widened / length, length)


def against(left, right):
    return lax.dot_general(
        left, right, (((1,), (1,)), ((), ())), preferred_element_type=jnp.float32
    )


def across_rows(left, right):
    return lax.dot_general(
        left, right, (((0,), (0,)), ((), ())), preferred_element_type=jnp.float32
    )


def on_device(teacher_new, queue, student, prototypes, owners, queue_oldest_slot):
    n_sample = lax.axis_size("sample")
    n_proto = lax.axis_size("proto")
    protos_total = K_DEV * n_proto
    teachers_total = (NEW_DEV + QUEUE_PER_INDEX) * n_sample
    new_total = NEW_DEV * n_sample
    my_index = lax.axis_index("sample")
    teacher_hat = unit_rows(jnp.concatenate([teacher_new, queue], 0))[0].astype(jnp.bfloat16)
    proto_unit, proto_length = unit_rows(prototypes)
    proto_hat = proto_unit.astype(jnp.bfloat16)
    student_normalized = unit_rows(student)[0].astype(jnp.bfloat16)
    logits = against(student_normalized, proto_hat) / student_temp
    exp_logits = jnp.exp(logits)
    denominator = lax.psum(jnp.sum(exp_logits, axis=1), "proto")
    exp_scores = jnp.exp(against(teacher_hat, proto_hat) / teacher_temp)
    row_scale = jnp.ones((exp_scores.shape[0],), jnp.float32)
    proto_scale = jnp.ones((K_DEV,), jnp.float32)
    for iteration in range(ITERS):
        column_sums = lax.psum(
            jnp.dot(row_scale, exp_scores, precision=lax.Precision.HIGHEST), "sample"
        )
        proto_scale = 1.0 / (protos_total * column_sums)
        row_totals = lax.psum(
            jnp.dot(exp_scores, proto_scale, precision=lax.Precision.HIGHEST), "proto"
        )
        row_scale = 1.0 / (teachers_total * row_totals)
    targets = (
        exp_scores[:NEW_DEV] * proto_scale[None, :] * row_scale[:NEW_DEV, None] * teachers_total
    )
    local_loss = jnp.sum(jnp.log(denominator)) / n_proto - jnp.sum(targets * logits)
    loss = lax.psum(local_loss, ("proto", "sample")) / new_total
    softmax_output = exp_logits / denominator[:, None]
    grad_scale = protos_total * NEW_DEV // 32
    logit_gradient = (grad_scale * (softmax_output - targets) / (new_total * student_temp)).astype(
        jnp.bfloat16
    )
    share = K_DEV // n_sample
    unit_gradient = lax.psum_scatter(
        across_rows(logit_gradient, student_normalized), "sample", scatter_dimension=0, tiled=True
    )
    my_unit = lax.dynamic_slice_in_dim(proto_unit, my_index * share, share, 0)
    my_length = lax.dynamic_slice_in_dim(proto_length, my_index * share, share, 0)
    proto_grad = (
        unit_gradient - my_unit * jnp.sum(my_unit * unit_gradient, axis=1, keepdims=True)
    ) / my_length
    my_head = queue_oldest_slot[0]
    owner_list = owners[:, 0]
    owner_range = jnp.arange(n_sample, dtype=jnp.int32)
    rows_all, owners_all = (
        lax.all_gather(teacher_new, "sample", axis=0, tiled=True),
        lax.all_gather(owner_list, "sample", axis=0, tiled=True),
    )
    onehot = (owners_all[:, None] == owner_range[None, :]).astype(jnp.int32)
    ranks = jnp.sum((jnp.cumsum(onehot, axis=0) - onehot) * onehot, axis=1)
    slot_index = jnp.where(
        owners_all == my_index, (my_head + ranks) % QUEUE_PER_INDEX, QUEUE_PER_INDEX
    )
    new_queue = queue.at[slot_index].set(rows_all, mode="drop")
    return (new_queue, proto_grad, loss)


def solution(mesh):
    in_specs = (
        P("sample", None),
        P("sample", None),
        P("sample", None),
        P("proto", None),
        P("sample", None),
        P("sample"),
    )
    out_specs = (P("sample", None), P(("proto", "sample"), None), P())
    return jax.shard_map(
        on_device, mesh=mesh, in_specs=in_specs, out_specs=out_specs, check_vma=False
    )
```

profile of v0, /device:TPU:0, one launch (start us, length us, event | category | flops | bytes accessed | tf_op | source)
XLA Modules:
  0.0 276.2 jit_solution(3856830147203164329)
XLA Ops:
  8.4 1.8 fusion
  10.5 2.6 multiply_exponential_fusion
  13.1 4.0 %fusion.17 = f32[1,2048]{1,0:T(1,128)S(1)} fusion(f32[1024,2048]{1,0:T(8,128)S(1)} %multiply_exponential_fusion), kind=kOutput, calls=%fused_computation.46 | convolution fusion | flops 25165824 | bytes 8396800 | tf_op jit(solution)/shard_map/dot_general | solution.py:54
  17.2 5.9 %psum.57 = f32[2048]{0:T(1024)S(1)} all-reduce(f32[2048]{0:T(1024)S(1)} %bitcast.50), channel_id=1, replica_groups=mesh['proto'=16,'sample'=2] {'sample'}, use_global_device_ids=true, to_apply=%region_9.0 | all-reduce | flops 2048 | bytes 16384 | tf_op jit(solution)/shard_map/psum | solution.py:53
  23.1 9.4 %fusion.25 = f32[1,1024]{1,0:T(1,128)S(1)} fusion(f32[1024,2048]{1,0:T(8,128)} %copy-done, f32[2048,1]{0,1:T(1,128)S(1)} %bitcast.46), kind=kOutput, calls=%fused_computation.55 | convolution fusion | flops 25165824 | bytes 8400896 | tf_op jit(solution)/shard_map/dot_general | solution.py:58
  32.5 33.0 %psum.58 = f32[1024]{0:T(1024)S(1)} all-reduce(f32[1024]{0:T(1024)S(1)} %bitcast.54), channel_id=1, replica_groups=mesh['proto'=16,'sample'=2] {'proto'}, use_global_device_ids=true, to_apply=%region_10.0 | all-reduce | flops 1024 | bytes 8192 | tf_op jit(solution)/shard_map/psum | solution.py:57
  65.5 6.3 %fusion.26 = f32[1,2048]{1,0:T(1,128)S(1)} fusion(f32[1024,1]{0,1:T(1,128)S(1)} %bitcast.55, f32[1024,2048]{1,0:T(8,128)} %copy-done), kind=kOutput, calls=%fused_computation.56 | convolution fusion | flops 25165824 | bytes 8400896 | tf_op jit(solution)/shard_map/dot_general | solution.py:54
  71.8 5.0 %psum.59 = f32[2048]{0:T(1024)S(1)} all-reduce(f32[2048]{0:T(1024)S(1)} %bitcast.47), channel_id=1, replica_groups=mesh['proto'=16,'sample'=2] {'sample'}, use_global_device_ids=true, to_apply=%region_11.0 | all-reduce | flops 2048 | bytes 16384 | tf_op jit(solution)/shard_map/psum | solution.py:53
  76.8 9.4 %fusion.27 = f32[1,1024]{1,0:T(1,128)S(1)} fusion(f32[1024,2048]{1,0:T(8,128)} %copy-done, f32[2048,1]{0,1:T(1,128)S(1)} %bitcast.48), kind=kOutput, calls=%fused_computation.57 | convolution fusion | flops 25165824 | bytes 8400896 | tf_op jit(solution)/shard_map/dot_general | solution.py:58
  86.2 29.5 %psum.60 = f32[1024]{0:T(1024)S(1)} all-reduce(f32[1024]{0:T(1024)S(1)} %bitcast.56), channel_id=1, replica_groups=mesh['proto'=16,'sample'=2] {'proto'}, use_global_device_ids=true, to_apply=%region_12.0 | all-reduce | flops 1024 | bytes 8192 | tf_op jit(solution)/shard_map/psum | solution.py:57
  115.7 6.3 %fusion.28 = f32[1,2048]{1,0:T(1,128)S(1)} fusion(f32[1024,1]{0,1:T(1,128)S(1)} %bitcast.57, f32[1024,2048]{1,0:T(8,128)} %copy-done), kind=kOutput, calls=%fused_computation.58 | convolution fusion | flops 25165824 | bytes 8400896 | tf_op jit(solution)/shard_map/dot_general | solution.py:54
  122.1 5.0 %psum.61 = f32[2048]{0:T(1024)S(1)} all-reduce(f32[2048]{0:T(1024)S(1)} %bitcast.49), channel_id=1, replica_groups=mesh['proto'=16,'sample'=2] {'sample'}, use_global_device_ids=true, to_apply=%region_13.0 | all-reduce | flops 2048 | bytes 16384 | tf_op jit(solution)/shard_map/psum | solution.py:53
  127.1 9.4 %fusion.29 = f32[1,1024]{1,0:T(1,128)S(1)} fusion(f32[1024,2048]{1,0:T(8,128)} %copy-done, f32[2048,1]{0,1:T(1,128)S(1)} %bitcast.45), kind=kOutput, calls=%fused_computation.59 | convolution fusion | flops 25165824 | bytes 8400896 | tf_op jit(solution)/shard_map/dot_general | solution.py:58
  136.5 29.5 %psum.62 = f32[1024]{0:T(1024)S(1)} all-reduce(f32[1024]{0:T(1024)S(1)} %bitcast.58), channel_id=1, replica_groups=mesh['proto'=16,'sample'=2] {'proto'}, use_global_device_ids=true, to_apply=%region_14.0 | all-reduce | flops 1024 | bytes 8192 | tf_op jit(solution)/shard_map/psum | solution.py:57
  166.1 4.2 %multiply_reduce_fusion = (f32[]{:T(128)}, f32[256]{0:T(256)S(1)}, f32[256,2048]{1,0:T(8,128)}) fusion(f32[1024,2048]{1,0:T(8,128)} %copy-done, f32[256]{0:T(256)S(1)} %slice.15, f32[2048]{0:T(1024)S(1)} %multiply_divide_fusion, f32[2048]{0:T(1024)S(1)} %add_sqrt_fusion, bf16[2048,384]{1,0:T(8,128)(2,1)S(1)} %copy-done.3, ...), kind=kOutput, calls=%fused_computation.9 | convolution fusion | flops 408977152 | bytes 5983236 | tf_op jit(solution)/shard_map/dot_general | solution.py:24
  170.3 29.7 %psum.56 = f32[256]{0:T(256)S(1)} all-reduce(f32[256]{0:T(256)S(1)} %get-tuple-element.4), channel_id=1, replica_groups=mesh['proto'=16,'sample'=2] {'proto'}, use_global_device_ids=true, to_apply=%region_7.0 | all-reduce | flops 256 | bytes 2048 | tf_op jit(solution)/shard_map/psum | solution.py:48
  200.0 5.1 %fusion.5 = f32[2048,384]{1,0:T(8,128)} fusion(f32[256,2048]{1,0:T(8,128)} %get-tuple-element.5, f32[1024,2048]{1,0:T(8,128)} %copy-done, f32[256]{0:T(256)S(1)} %slice.15, f32[2048]{0:T(1024)S(1)} %multiply_divide_fusion, f32[256]{0:T(256)S(1)} %psum.56, bf16[256,384]{1,0:T(8,128)(2,1)S(1)} %copy-done.5, f32[256]{0:T(256)S(1)} %add_sqrt_fusion.2), kind=kOutput, calls=%fused_computation.18 | convolution fusion | flops 406618112 | bytes 7547904 | tf_op jit(solution)/shard_map/dot_general | solution.py:30
  207.0 37.4 %psum.63 = f32[]{:T(128)} all-reduce(f32[]{:T(128)S(6)} %sub.15), channel_id=1, replica_groups=mesh['proto'=16,'sample'=2] {'proto','sample'}, use_global_device_ids=true, to_apply=%region_19.20 | all-reduce | flops 1 | bytes 8 | tf_op jit(solution)/shard_map/psum | solution.py:65
  244.4 4.6 %all-gather = s32[512,1]{0,1:T(1,128)S(1)} all-gather(s32[256,1]{0,1:T(1,128)S(1)} %copy-done.7), channel_id=2, replica_groups=mesh['proto'=16,'sample'=2] {'sample'}, dimensions={0}, use_global_device_ids=true | all-gather | bytes 3072 | tf_op jit(solution)/shard_map/all_gather | solution.py:85
  251.3 6.4 %all_gather.7 = bf16[512,384]{1,0:T(8,128)(2,1)S(1)} all-gather(bf16[256,384]{1,0:T(8,128)(2,1)S(1)} %copy-done.4), channel_id=1, replica_groups=mesh['proto'=16,'sample'=2] {'sample'}, dimensions={0}, use_global_device_ids=true | all-gather | bytes 589824 | tf_op jit(solution)/shard_map/all_gather | solution.py:84
  257.7 2.7 scatter_fusion
  260.4 2.0 convert_divide_fusion
  262.5 2.3 multiply_reduce_fusion.1
  265.3 2.9 %subtract_divide_fusion = f32[1024,384]{1,0:T(8,128)} fusion(f32[1024,384]{1,0:T(8,128)} %reduce-scatter.2.cloned.1.call-done, f32[2048,384]{1,0:T(8,128)S(1)} %copy-done.2, s32[]{:T(128)} %select_n.21, f32[1024]{0:T(1024)S(1)} %dynamic-slice-done, f32[1024]{0:T(1024)S(1)} %multiply_reduce_fusion.1), kind=kLoop, calls=%fused_computation.16 | loop fusion | flops 1179648 | bytes 4726788 | tf_op jit(solution)/shard_map/div | solution.py:77
  (42 shorter events, 4.0 us)
Async XLA Ops:
  7.2 3.1 %copy-start.4 = (bf16[256,384]{1,0:T(8,128)(2,1)S(1)}, bf16[256,384]{1,0:T(8,128)(2,1)}, u32[]{:S(2)}) copy-start(bf16[256,384]{1,0:T(8,128)(2,1)} %param.6) | copy-start | bytes 589828
  7.2 3.3 %copy-start.3 = (bf16[2048,384]{1,0:T(8,128)(2,1)S(1)}, bf16[2048,384]{1,0:T(8,128)(2,1)}, u32[]{:S(2)}) copy-start(bf16[2048,384]{1,0:T(8,128)(2,1)} %param.9) | copy-start | bytes 4718596
  7.2 255.3 %reduce-scatter.2.cloned.1.call-start = ((), (), s32[]{:S(2)}) async-start(), calls=%async_computation.1 | async-start | bytes 4718592 | tf_op jit(solution)/shard_map/reduce_scatter | solution.py:72
  10.2 250.2 %copy-start.6 = (f32[2048]{0:T(1024)}, f32[2048]{0:T(1024)S(1)}, u32[]{:S(2)}) copy-start(f32[2048]{0:T(1024)S(1)} %add_sqrt_fusion) | copy-start | bytes 24580
  13.1 4.0 %copy-start = (f32[1024,2048]{1,0:T(8,128)}, f32[1024,2048]{1,0:T(8,128)S(1)}, u32[]{:S(2)}) copy-start(f32[1024,2048]{1,0:T(8,128)S(1)} %multiply_exponential_fusion) | copy-start | bytes 25165828
  127.0 39.0 %copy-start.5 = (bf16[256,384]{1,0:T(8,128)(2,1)S(1)}, bf16[256,384]{1,0:T(8,128)(2,1)}, u32[]{:S(2)}) copy-start(bf16[256,384]{1,0:T(8,128)(2,1)} %param.8) | copy-start | bytes 589828
  205.1 39.3 %copy-start.7 = (s32[256,1]{0,1:T(1,128)S(1)}, s32[256,1]{0,1:T(1,128)}, u32[]{:S(2)}) copy-start(s32[256,1]{0,1:T(1,128)} %param.10) | copy-start | bytes 3076
  260.4 2.0 copy-start.1
  262.5 2.3 dynamic-slice-start
  262.5 2.8 %copy-start.2 = (f32[2048,384]{1,0:T(8,128)S(1)}, f32[2048,384]{1,0:T(8,128)}, u32[]{:S(2)}) copy-start(f32[2048,384]{1,0:T(8,128)} %convert_divide_fusion) | copy-start | bytes 9437188
Sparse Core Ops, SparseCore 0:
  205.2 42.0 reduce-scatter.1
where the time goes:
time: 277 us; the launch traced here: 276 us
  blocking collectives  186 us (67%)
  matrix products  56.8 us (21%)
  between operations  17.9 us (6%)
  other arithmetic  10.9 us (4%)
  local copies, waits for them, and re-layouts  4.7 us (2%)
    psum x3, blocking collectives, on_device(): lax.psum(jnp.dot(exp_scores, proto_scale, precision=lax.Precision.HIGHEST...  92 us
    psum x1, blocking collectives, on_device(): loss = lax.psum(local_loss, ('proto', 'sample')) / new_total  37.4 us
    psum x1, blocking collectives, on_device(): denominator = lax.psum(jnp.sum(exp_logits, axis=1), 'proto')  29.7 us
    dot_general x3, matrix products, on_device(): jnp.dot(exp_scores, proto_scale, precision=lax.Precision.HIGHEST)  28.2 us
    dot_general x3, matrix products, on_device(): jnp.dot(row_scale, exp_scores, precision=lax.Precision.HIGHEST)  16.7 us
    psum x3, blocking collectives, on_device(): lax.psum(jnp.dot(row_scale, exp_scores, precision=lax.Precision.HIGHEST),...  15.9 us
    dot_general x2, matrix products, against(): lax.dot_general(left, right, (((1,), (1,)), ((), ())), preferred_element_...  6.8 us
    all_gather x1, blocking collectives, on_device(): lax.all_gather(teacher_new, 'sample', axis=0, tiled=True)  6.36 us
  transfers between devices with their start and end apart: 1, of which 0 were waited for; matrix products, arithmetic and copies ran while one was open for 2% of the time, Pallas kernels for 0%

commit v1 on v0

v1 whole, which is shorter than its diff:
```python
import functools
import math

import jax
import jax.numpy as jnp
from jax import lax
from jax.experimental import pallas as pl
from jax.experimental.pallas import tpu as pltpu
from jax.sharding import PartitionSpec as P

ITERS = 3
LANES = 128
teacher_temp = 0.07
student_temp = 0.1
epsilon = 1e-12
LOG2E = math.log2(math.e)

f32, bf16 = jnp.float32, jnp.bfloat16
MESH = pl.DeviceIdType.MESH


def nt(left, right):
    return lax.dot_general(left, right, (((1,), (1,)), ((), ())), preferred_element_type=f32)


def nn(left, right):
    return lax.dot_general(left, right, (((1,), (0,)), ((), ())), preferred_element_type=f32)


def unit_rows(values):
    wide = values.astype(f32)
    squares = jnp.sum(wide * wide, axis=1, keepdims=True) + epsilon
    return wide * lax.rsqrt(squares)


def to_lanes(tile, first, rows):
    return jnp.concatenate([tile[r : r + 1, :] for r in range(first, first + rows)], axis=1)


def to_rows(vector):
    return [vector[:, c : c + LANES] for c in range(0, vector.shape[1], LANES)]


def padded(pieces, rows):
    have = sum(p.shape[0] for p in pieces)
    if have < rows:
        pieces = pieces + [jnp.zeros((rows - have, LANES), f32)]
    return jnp.concatenate(pieces, axis=0)


def high_low(vector):
    high = vector.astype(bf16).astype(f32)
    row = lax.broadcasted_iota(jnp.int32, (16, vector.shape[1]), 0)
    return jnp.where(row == 0, high, jnp.where(row == 1, vector - high, 0.0)).astype(bf16)


def joined(product):
    return product[0:1, :] + product[1:2, :]


def round8(n):
    return -(-n // 8) * 8


def wrap(index, n):
    return jnp.where(index >= n, index - n, index)


def kernel(
    n_proto, n_sample,
    tn_ref, q_ref, st_ref, pr_ref, ow_ref, head_ref,
    nq_ref, pg_ref, loss_ref,
    that, phat, sthat, es, bulk, stall, thall, y0buf, ybuf, rbuf, zbuf, pst, pscol, expl, uval,
    y0_send, y0_recv, y_send, y_recv, r_send, r_recv, z_send, z_recv,
    b_send, b_recv, w_send, w_recv,
):
    new, feat = tn_ref.shape
    ql = q_ref.shape[0]
    kdev = pr_ref.shape[0]
    tdev = new + ql
    half = new // 2
    nb, tb, kb = new // LANES, tdev // LANES, kdev // LANES
    share = kdev // n_sample
    n_new = new * n_sample
    protos_total = kdev * n_proto
    teachers_total = float(tdev * n_sample)
    blk = min(256, share)
    me_p, me_s = lax.axis_index("proto"), lax.axis_index("sample")
    core = lax.rem(me_p, 2)
    sibling = me_p + 1 - 2 * core

    def p_peers():
        return [wrap(me_p + d, n_proto) for d in range(1, n_proto)]

    def s_peers():
        return [wrap(me_s + d, n_sample) for d in range(1, n_sample)]

    barrier = pltpu.get_barrier_semaphore()
    for p in p_peers():
        pl.semaphore_signal(barrier, inc=1, device_id={"proto": p}, device_id_type=MESH)
    for s in s_peers():
        pl.semaphore_signal(barrier, inc=1, device_id={"sample": s}, device_id_type=MESH)

    def send_s(src, dst, ssem, rsem):
        for s in s_peers():
            pltpu.make_async_remote_copy(src, dst, ssem, rsem, device_id={"sample": s}, device_id_type=MESH).start()

    def send_p(src, dst, ssem, rsem):
        for p in p_peers():
            pltpu.make_async_remote_copy(src, dst, ssem, rsem, device_id={"proto": p}, device_id_type=MESH).start()

    def whole(ref, count, ssem, rsem):
        view = ref.at[pl.ds(0, count)]
        return pltpu.make_async_remote_copy(view, view, ssem, rsem, device_id={"proto": sibling}, device_id_type=MESH)

    student = unit_rows(st_ref[...]).astype(bf16)
    sthat[...] = student
    for h in range(2):
        bulk[me_s, h, 0] = student[h * half : (h + 1) * half]
        bulk[me_s, h, 1] = tn_ref[h * half : (h + 1) * half, :]

    that[0:new, :] = unit_rows(tn_ref[...]).astype(bf16)
    that[new:tdev, :] = unit_rows(q_ref[...]).astype(bf16)

    pl.semaphore_wait(barrier, n_proto - 1 + n_sample - 1)
    for d in range(1, n_sample):
        pltpu.make_async_remote_copy(
            bulk.at[me_s, core], bulk.at[me_s, core], b_send.at[d], b_recv.at[d],
            device_id={"sample": wrap(me_s + d, n_sample)}, device_id_type=MESH,
        ).start()

    pb = 256

    def score_block(b, carry):
        at = pl.multiple_of(b * pb, pb)
        unit = unit_rows(pr_ref[pl.ds(at, pb), :]).astype(bf16)
        phat[pl.ds(at, pb), :] = unit
        e = jnp.exp2(nt(that[...], unit) * (LOG2E / teacher_temp))
        es[new:, pl.ds(at, pb)] = e.astype(bf16)
        sums = jnp.sum(e, axis=0, keepdims=True)
        for c, row in enumerate(to_rows(sums)):
            y0buf[me_s, pl.ds(b * (pb // LANES) + c, 1), :] = row
        return carry

    lax.fori_loop(0, kdev // pb, score_block, 0)
    y0buf[me_s, kb:, :] = padded([ow_ref[...].astype(f32)], round8(nb))
    send_s(y0buf.at[me_s], y0buf.at[me_s], y0_send, y0_recv)

    def student_block(b, denominator):
        at = pl.multiple_of(b * pb, pb)
        unit = phat[pl.ds(at, pb), :]
        logits = nt(sthat[...], unit) * (1.0 / student_temp)
        es[0:new, pl.ds(at, pb)] = (es[new : 2 * new, pl.ds(at, pb)].astype(f32) * logits).astype(bf16)
        across = nt(unit, sthat[...]) * (LOG2E / student_temp)
        return denominator + jnp.sum(jnp.exp2(across), axis=0, keepdims=True)

    denominator = lax.fori_loop(0, kdev // pb, student_block, jnp.zeros((1, new), f32))

    whole(y0buf, n_sample - 1, y0_send, y0_recv).wait_recv()
    columns = jnp.sum(y0buf[:, 0:kb, :], axis=0)
    scale_tile = 1.0 / (float(protos_total) * columns)

    def row_totals(tile, first, rows):
        left = high_low(to_lanes(tile, 0, kb))
        return jnp.concatenate([joined(nt(left, es[r : r + 256, :])) for r in range(first, first + rows, 256)], axis=1)

    def column_sums(tile):
        left = high_low(to_lanes(tile, 0, tb))
        return jnp.concatenate([joined(nn(left, es[new:, c : c + 256])) for c in range(0, kdev, 256)], axis=1)

    def gather_new():
        for s in range(n_sample):
            for h in range(2):
                at = s * new + h * half
                stall[at : at + half, :] = bulk[s, h, 0]
                thall[at : at + half, :] = unit_rows(bulk[s, h, 1]).astype(bf16)

    def refill():
        head = head_ref[0].astype(f32)
        before = lax.broadcasted_iota(jnp.int32, (LANES, LANES), 0) < lax.broadcasted_iota(jnp.int32, (LANES, LANES), 1)
        before = before.astype(f32).astype(bf16)
        slots = lax.broadcasted_iota(jnp.int32, (ql, LANES), 0)
        mine = me_s.astype(f32)
        offset = jnp.zeros((1, 1), f32)
        rows = jnp.zeros((ql, feat), f32)
        hit = jnp.zeros((ql, 1), f32)
        per_half = nb // 2
        for s in range(n_sample):
            for c in range(nb):
                own = (y0buf[s, kb + c : kb + c + 1, :] == mine).astype(f32)
                rank = nn(jnp.broadcast_to(own, (16, LANES)).astype(bf16), before)[0:1, :] + offset
                offset = offset + jnp.sum(own, axis=1, keepdims=True)
                slot = head + rank
                slot = jnp.where(slot >= float(ql), slot - float(ql), slot)
                slot = jnp.where(own > 0.0, slot, -1.0).astype(jnp.int32)
                chosen = (slots == slot).astype(f32)
                hit = hit + jnp.sum(chosen, axis=1, keepdims=True)
                h, inner = c // per_half, (c % per_half) * LANES
                rows = rows + nn(chosen.astype(bf16), bulk[s, h, 1, inner : inner + LANES, :])
        nq_ref[...] = jnp.where(hit > 0.0, rows, q_ref[...].astype(f32)).astype(bf16)

    first_row = pl.multiple_of(me_s * share, share)

    def own_block(b, carry):
        at = pl.multiple_of(b * blk, blk)
        unit = phat[pl.ds(first_row + at, blk), :]
        for s in range(n_sample):
            span = slice(s * new, (s + 1) * new)
            expl[pl.ds(at, blk), span] = jnp.exp2(nt(unit, stall[span, :]) * (LOG2E / student_temp))
            uval[pl.ds(at, blk), span] = jnp.exp2(nt(unit, thall[span, :]) * (LOG2E / teacher_temp))
        return carry

    for step in range(ITERS - 1):
        totals = row_totals(scale_tile, new, tdev)
        rbuf[step, me_p] = padded(to_rows(totals), tb)
        send_p(rbuf.at[step, me_p], rbuf.at[step, me_p], r_send.at[step], r_recv.at[step])
        if step == 0:
            for d in range(1, n_sample):
                s = wrap(me_s + n_sample - d, n_sample)
                arrived = bulk.at[s, core]
                pltpu.make_async_remote_copy(arrived, arrived, b_send.at[d], b_recv.at[d], device_id={"proto": sibling}, device_id_type=MESH).wait_recv()
                pltpu.make_async_remote_copy(arrived, arrived, w_send.at[d], w_recv.at[d], device_id={"proto": sibling}, device_id_type=MESH).start()
        else:
            for d in range(1, n_sample):
                s = wrap(me_s + n_sample - d, n_sample)
                other = bulk.at[s, 1 - core]
                pltpu.make_async_remote_copy(other, other, w_send.at[d], w_recv.at[d], device_id={"proto": sibling}, device_id_type=MESH).wait_recv()
            gather_new()
            refill()
        whole(rbuf.at[step], n_proto - 1, r_send.at[step], r_recv.at[step]).wait_recv()
        row_tile = 1.0 / (teachers_total * jnp.sum(rbuf[step], axis=0))
        ybuf[step, me_s] = padded(to_rows(column_sums(row_tile)), kb)
        send_s(ybuf.at[step, me_s], ybuf.at[step, me_s], y_send.at[step], y_recv.at[step])
        if step == ITERS - 2:
            lax.fori_loop(0, share // blk, own_block, 0)
        whole(ybuf.at[step], n_sample - 1, y_send.at[step], y_recv.at[step]).wait_recv()
        scale_tile = 1.0 / (float(protos_total) * jnp.sum(ybuf[step], axis=0))

    totals = row_totals(scale_tile, 0, 2 * new)
    last = padded(to_rows(totals) + to_rows(denominator), rbuf.shape[2])
    final = ITERS - 1
    rbuf[final, me_p] = last
    send_p(rbuf.at[final, me_p], rbuf.at[final, me_p], r_send.at[final], r_recv.at[final])

    pst[...] = scale_tile
    for r in range(share // LANES):
        row = pst[pl.ds(me_s * (share // LANES) + r, 1), :]
        pscol[r * LANES : (r + 1) * LANES, :] = jnp.transpose(jnp.broadcast_to(row, (LANES, LANES)))

    def scale_block(b, carry):
        at = pl.multiple_of(b * blk, blk)
        column = pscol[pl.ds(at, blk), :]
        for c in range(0, n_new, LANES):
            uval[pl.ds(at, blk), c : c + LANES] = uval[pl.ds(at, blk), c : c + LANES] * column
        return carry

    lax.fori_loop(0, share // blk, scale_block, 0)

    whole(rbuf.at[final], n_proto - 1, r_send.at[final], r_recv.at[final]).wait_recv()
    summed = jnp.sum(rbuf[final], axis=0)
    scaled = 1.0 / summed[nb : 2 * nb, :]
    denominators = summed[2 * nb : 3 * nb, :]
    cross = jnp.log(denominators) - scaled * summed[0:nb, :]
    cross = jnp.sum(jnp.sum(cross, axis=0, keepdims=True), axis=1, keepdims=True)
    grad_scale = float(protos_total * new // 32) / (n_new * student_temp)
    zbuf[me_s] = padded(
        [grad_scale * scaled, grad_scale / denominators, jnp.broadcast_to(cross, (1, LANES))],
        zbuf.shape[1],
    )
    send_s(zbuf.at[me_s], zbuf.at[me_s], z_send, z_recv)
    whole(zbuf, n_sample - 1, z_send, z_recv).wait_recv()
    terms = zbuf[...]
    loss = terms[0, 2 * nb : 2 * nb + 1, 0:1]
    for s in range(1, n_sample):
        loss = loss + terms[s, 2 * nb : 2 * nb + 1, 0:1]
    loss_ref[...] = loss / float(n_new)
    row_scale = jnp.concatenate([to_lanes(terms[s], 0, nb) for s in range(n_sample)], axis=1)
    soft_scale = jnp.concatenate([to_lanes(terms[s], nb, nb) for s in range(n_sample)], axis=1)

    def gradient_block(b, carry):
        at = pl.multiple_of(b * blk, blk)
        rows = pl.ds(at, blk)
        gradient = (expl[rows, :] * soft_scale - uval[rows, :] * row_scale).astype(bf16)
        unit_gradient = nn(gradient, stall[...])
        wide = pr_ref[pl.ds(first_row + at, blk), :].astype(f32)
        inverse = lax.rsqrt(jnp.sum(wide * wide, axis=1, keepdims=True) + epsilon)
        unit = wide * inverse
        along = jnp.sum(unit * unit_gradient, axis=1, keepdims=True)
        pg_ref[rows, :] = (unit_gradient - unit * along) * inverse
        return carry

    lax.fori_loop(0, share // blk, gradient_block, 0)

    whole(y0buf, n_sample - 1, y0_send, y0_recv).wait_send()
    for step in range(ITERS - 1):
        whole(ybuf.at[step], n_sample - 1, y_send.at[step], y_recv.at[step]).wait_send()
    for step in range(ITERS):
        whole(rbuf.at[step], n_proto - 1, r_send.at[step], r_recv.at[step]).wait_send()
    whole(zbuf, n_sample - 1, z_send, z_recv).wait_send()
    for d in range(1, n_sample):
        mine = bulk.at[me_s, core]
        pltpu.make_async_remote_copy(mine, mine, b_send.at[d], b_recv.at[d], device_id={"proto": sibling}, device_id_type=MESH).wait_send()
        pltpu.make_async_remote_copy(mine, mine, w_send.at[d], w_recv.at[d], device_id={"proto": sibling}, device_id_type=MESH).wait_send()


def on_device(n_proto, n_sample, teacher_new, queue, student, prototypes, owners, queue_oldest_slot):
    new, feat = teacher_new.shape
    ql, kdev = queue.shape[0], prototypes.shape[0]
    tdev = new + ql
    nb, tb, kb = new // LANES, tdev // LANES, kdev // LANES
    share = kdev // n_sample
    n_new = new * n_sample
    vmem = pl.BlockSpec(memory_space=pltpu.VMEM)
    smem = pl.BlockSpec(memory_space=pltpu.SMEM)
    dma = pltpu.SemaphoreType.DMA
    rows = max(round8(tb), round8(3 * nb))
    new_queue, proto_grad, loss = pl.pallas_call(
        functools.partial(kernel, n_proto, n_sample),
        out_shape=(
            jax.ShapeDtypeStruct((ql, feat), bf16),
            jax.ShapeDtypeStruct((share, feat), f32),
            jax.ShapeDtypeStruct((1, 1), f32),
        ),
        in_specs=[vmem] * 5 + [smem],
        out_specs=(vmem, vmem, vmem),
        scratch_shapes=[
            pltpu.VMEM((tdev, feat), bf16),
            pltpu.VMEM((kdev, feat), bf16),
            pltpu.VMEM((new, feat), bf16),
            pltpu.VMEM((new + tdev, kdev), bf16),
            pltpu.VMEM((n_sample, 2, 2, new // 2, feat), bf16),
            pltpu.VMEM((n_new, feat), bf16),
            pltpu.VMEM((n_new, feat), bf16),
            pltpu.VMEM((n_sample, kb + round8(nb), LANES), f32),
            pltpu.VMEM((ITERS - 1, n_sample, kb, LANES), f32),
            pltpu.VMEM((ITERS, n_proto, rows, LANES), f32),
            pltpu.VMEM((n_sample, round8(2 * nb + 1), LANES), f32),
            pltpu.VMEM((kb, LANES), f32),
            pltpu.VMEM((share, LANES), f32),
            pltpu.VMEM((share, n_new), f32),
            pltpu.VMEM((share, n_new), f32),
            dma, dma,
            dma((ITERS - 1,)), dma((ITERS - 1,)),
            dma((ITERS,)), dma((ITERS,)),
            dma, dma,
            dma((n_sample,)), dma((n_sample,)),
            dma((n_sample,)), dma((n_sample,)),
        ],
        compiler_params=pltpu.CompilerParams(
            collective_id=0, has_side_effects=True, vmem_limit_bytes=48 * 1024 * 1024
        ),
    )(teacher_new, queue, student, prototypes, owners.reshape(nb, LANES), queue_oldest_slot)
    return new_queue, proto_grad, loss.reshape(())


def solution(mesh):
    in_specs = (
        P("sample", None),
        P("sample", None),
        P("sample", None),
        P("proto", None),
        P("sample", None),
        P("sample"),
    )
    out_specs = (P("sample", None), P(("proto", "sample"), None), P())
    body = functools.partial(on_device, mesh.shape["proto"], mesh.shape["sample"])
    return jax.shard_map(body, mesh=mesh, in_specs=in_specs, out_specs=out_specs, check_vma=False)
```

time: 277 us -> 49.9 us (0.18)
  blocking collectives: 186 us -> 0 us
  matrix products: 56.8 us -> 0 us
  Pallas kernels: 0 us -> 39.7 us
  between operations: 17.9 us -> 2.99 us
  other arithmetic: 10.9 us -> 0 us
    psum x8 -> x0, blocking collectives: 175 us -> none  [the longest x3 92 us: on_device(): lax.psum(jnp.dot(exp_scores, proto_scale, precision=lax.Precision.HIGHEST...]
    dot_general x9 -> x0, matrix products: 56.8 us -> none  [the longest x3 28.2 us: on_device(): jnp.dot(exp_scores, proto_scale, precision=lax.Precision.HIGHEST)]
    pallas_call x0 -> x1, Pallas kernels: none -> 39.7 us  [on_device(): pl.pallas_call(functools.partial(kernel, n_proto, n_sample), out_shape=(j...]
    all_gather x2 -> x0, blocking collectives: 10.9 us -> none  [the longest x1 6.36 us: on_device(): lax.all_gather(teacher_new, 'sample', axis=0, tiled=True)]
    unnamed x17 -> x12, local copies, waits for them, and re-layouts: 1.8 us -> 6.96 us
    reduce_sum x6 -> x0, other arithmetic: 5.01 us -> none  [the longest x1 2.25 us: on_device(): jnp.sum(my_unit * unit_gradient, axis=1, keepdims=True)]
    div x8 -> x0, other arithmetic: 4.98 us -> none  [the longest x1 2.93 us: on_device(): (unit_gradient - my_unit * jnp.sum(my_unit * unit_gradient, axis=1, keepd...]
  transfers between devices with their start and end apart: 1 -> 0, of which waited for: 0 -> 0; matrix products, arithmetic and copies ran while one was open for 2% -> 0% of each run, Pallas kernels for 0% -> 0%
where the time goes in v1:
time: 49.9 us; the launch traced here: 49.6 us
  Pallas kernels  39.7 us (80%)
  local copies, waits for them, and re-layouts  6.96 us (14%)
  between operations  2.99 us (6%)
    pallas_call x1, Pallas kernels, on_device(): pl.pallas_call(functools.partial(kernel, n_proto, n_sample), out_shape=(j...  39.7 us
    unnamed x12, local copies, waits for them, and re-layouts  6.96 us

profile of v1, /device:TPU:0, one launch (start us, length us, event | category | flops | bytes accessed | tf_op | source)
XLA Modules:
  0.0 49.6 jit_solution(14681584129488821346)
XLA Ops:
  1.3 0.0 copy-start
  1.3 1.4 %copy-done = bf16[2048,384]{1,0:T(8,128)(2,1)S(1)} copy-done((bf16[2048,384]{1,0:T(8,128)(2,1)S(1)}, bf16[2048,384]{1,0:T(8,128)(2,1)}, u32[]{:S(2)}) %copy-start) | copy-done | bytes 1572888
  2.7 0.0 copy-start.1
  2.7 1.1 %copy-done.1 = bf16[768,384]{1,0:T(8,128)(2,1)S(1)} copy-done((bf16[768,384]{1,0:T(8,128)(2,1)S(1)}, bf16[768,384]{1,0:T(8,128)(2,1)}, u32[]{:S(2)}) %copy-start.1) | copy-done | bytes 589848
  3.8 0.0 copy-start.2
  3.8 0.9 %copy-done.2 = bf16[256,384]{1,0:T(8,128)(2,1)S(1)} copy-done((bf16[256,384]{1,0:T(8,128)(2,1)S(1)}, bf16[256,384]{1,0:T(8,128)(2,1)}, u32[]{:S(2)}) %copy-start.2) | copy-done | bytes 196632
  4.7 0.0 copy-start.3
  4.7 0.9 %copy-done.3 = bf16[256,384]{1,0:T(8,128)(2,1)S(1)} copy-done((bf16[256,384]{1,0:T(8,128)(2,1)S(1)}, bf16[256,384]{1,0:T(8,128)(2,1)}, u32[]{:S(2)}) %copy-start.3) | copy-done | bytes 196632
  5.6 0.0 copy-start.4
  5.6 0.7 %copy-done.4 = s32[256,1]{0,1:T(1,128)S(1)} copy-done((s32[256,1]{0,1:T(1,128)S(1)}, s32[256,1]{0,1:T(1,128)}, u32[]{:S(2)}) %copy-start.4) | copy-done | bytes 1048
  6.3 39.7 %shard_map.85 = (bf16[768,384]{1,0:T(8,128)(2,1)S(1)}, f32[1024,384]{1,0:T(8,128)S(1)}, f32[1,1]{1,0:T(1,128)}) custom-call(bf16[256,384]{1,0:T(8,128)(2,1)S(1)} %copy-done.2, bf16[768,384]{1,0:T(8,128)(2,1)S(1)} %copy-done.1, bf16[256,384]{1,0:T(8,128)(2,1)S(1)} %copy-done.3, bf16[2048,384]{1,0:T(8,128)(2,1)S(1)} %copy-done, s32[2,128]{1,0:T(2,128)S(1)} %bitcast.2, ...), custom_call_target="tpu_custom_call" | custom-call | tf_op jit(solution)/shard_map/pallas_call | solution.py:317
  46.0 0.8 %copy.13 = bf16[768,384]{1,0:T(8,128)(2,1)} copy(bf16[768,384]{1,0:T(8,128)(2,1)S(1)} %get-tuple-element.12) | data formatting | bytes 1179648
  46.8 1.1 %copy.14 = f32[1024,384]{1,0:T(8,128)} copy(f32[1024,384]{1,0:T(8,128)S(1)} %get-tuple-element.13) | data formatting | bytes 3145728
Async XLA Ops:
  1.3 1.4 %copy-start = (bf16[2048,384]{1,0:T(8,128)(2,1)S(1)}, bf16[2048,384]{1,0:T(8,128)(2,1)}, u32[]{:S(2)}) copy-start(bf16[2048,384]{1,0:T(8,128)(2,1)} %pr_ref.1) | copy-start | bytes 4718596
  2.7 1.1 %copy-start.1 = (bf16[768,384]{1,0:T(8,128)(2,1)S(1)}, bf16[768,384]{1,0:T(8,128)(2,1)}, u32[]{:S(2)}) copy-start(bf16[768,384]{1,0:T(8,128)(2,1)} %q_ref.1) | copy-start | bytes 1769476
  3.8 0.9 %copy-start.2 = (bf16[256,384]{1,0:T(8,128)(2,1)S(1)}, bf16[256,384]{1,0:T(8,128)(2,1)}, u32[]{:S(2)}) copy-start(bf16[256,384]{1,0:T(8,128)(2,1)} %tn_ref.1) | copy-start | bytes 589828
  4.7 0.9 %copy-start.3 = (bf16[256,384]{1,0:T(8,128)(2,1)S(1)}, bf16[256,384]{1,0:T(8,128)(2,1)}, u32[]{:S(2)}) copy-start(bf16[256,384]{1,0:T(8,128)(2,1)} %st_ref.1) | copy-start | bytes 589828
  5.6 0.7 %copy-start.4 = (s32[256,1]{0,1:T(1,128)S(1)}, s32[256,1]{0,1:T(1,128)}, u32[]{:S(2)}) copy-start(s32[256,1]{0,1:T(1,128)} %param.10) | copy-start | bytes 3076

commit v2 on v1

--- a/solution.py
+++ b/solution.py
@@ -68,8 +68,9 @@
 
 def kernel(
     n_proto, n_sample,
-    tn_ref, q_ref, st_ref, pr_ref, ow_ref, head_ref,
+    tn_hbm, q_hbm, st_hbm, pr_hbm, ow_hbm, head_ref,
     nq_ref, pg_ref, loss_ref,
+    tn_ref, q_ref, st_ref, pr_ref, ow_ref, in_sem,
     that, phat, sthat, es, bulk, stall, thall, y0buf, ybuf, rbuf, zbuf, pst, pscol, expl, uval,
     y0_send, y0_recv, y_send, y_recv, r_send, r_recv, z_send, z_recv,
     b_send, b_recv, w_send, w_recv,
@@ -95,6 +96,15 @@
     def s_peers():
         return [wrap(me_s + d, n_sample) for d in range(1, n_sample)]
 
+    arriving = [
+        pltpu.make_async_copy(there, here, in_sem.at[i])
+        for i, (there, here) in enumerate(
+            [(st_hbm, st_ref), (tn_hbm, tn_ref), (q_hbm, q_ref), (pr_hbm, pr_ref), (ow_hbm, ow_ref)]
+        )
+    ]
+    for copy in arriving:
+        copy.start()
+
     barrier = pltpu.get_barrier_semaphore()
     for p in p_peers():
         pl.semaphore_signal(barrier, inc=1, device_id={"proto": p}, device_id_type=MESH)
@@ -113,6 +123,8 @@
         view = ref.at[pl.ds(0, count)]
         return pltpu.make_async_remote_copy(view, view, ssem, rsem, device_id={"proto": sibling}, device_id_type=MESH)
 
+    arriving[0].wait()
+    arriving[1].wait()
     student = unit_rows(st_ref[...]).astype(bf16)
     sthat[...] = student
     for h in range(2):
@@ -120,8 +132,11 @@
         bulk[me_s, h, 1] = tn_ref[h * half : (h + 1) * half, :]
 
     that[0:new, :] = unit_rows(tn_ref[...]).astype(bf16)
+    arriving[2].wait()
     that[new:tdev, :] = unit_rows(q_ref[...]).astype(bf16)
 
+    arriving[3].wait()
+    arriving[4].wait()
     pl.semaphore_wait(barrier, n_proto - 1 + n_sample - 1)
     for d in range(1, n_sample):
         pltpu.make_async_remote_copy(
@@ -142,7 +157,7 @@
             y0buf[me_s, pl.ds(b * (pb // LANES) + c, 1), :] = row
         return carry
 
-    lax.fori_loop(0, kdev // pb, score_block, 0)
+    lax.fori_loop(0, kdev // pb, score_block, 0, unroll=2)
     y0buf[me_s, kb:, :] = padded([ow_ref[...].astype(f32)], round8(nb))
     send_s(y0buf.at[me_s], y0buf.at[me_s], y0_send, y0_recv)
 
@@ -289,7 +304,7 @@
         pg_ref[rows, :] = (unit_gradient - unit * along) * inverse
         return carry
 
-    lax.fori_loop(0, share // blk, gradient_block, 0)
+    lax.fori_loop(0, share // blk, gradient_block, 0, unroll=2 if share // blk > 1 else 1)
 
     whole(y0buf, n_sample - 1, y0_send, y0_recv).wait_send()
     for step in range(ITERS - 1):
@@ -321,9 +336,15 @@
             jax.ShapeDtypeStruct((share, feat), f32),
             jax.ShapeDtypeStruct((1, 1), f32),
         ),
-        in_specs=[vmem] * 5 + [smem],
+        in_specs=[pl.BlockSpec(memory_space=pltpu.HBM)] * 5 + [smem],
         out_specs=(vmem, vmem, vmem),
         scratch_shapes=[
+            pltpu.VMEM((new, feat), bf16),
+            pltpu.VMEM((ql, feat), bf16),
+            pltpu.VMEM((new, feat), bf16),
+            pltpu.VMEM((kdev, feat), bf16),
+            pltpu.VMEM((nb, LANES), jnp.int32),
+            dma((5,)),
             pltpu.VMEM((tdev, feat), bf16),
             pltpu.VMEM((kdev, feat), bf16),
             pltpu.VMEM((new, feat), bf16),
@@ -347,7 +368,7 @@
             dma((n_sample,)), dma((n_sample,)),
         ],
         compiler_params=pltpu.CompilerParams(
-            collective_id=0, has_side_effects=True, vmem_limit_bytes=48 * 1024 * 1024
+            collective_id=0, has_side_effects=True, vmem_limit_bytes=62 * 1024 * 1024
         ),
     )(teacher_new, queue, student, prototypes, owners.reshape(nb, LANES), queue_oldest_slot)
     return new_queue, proto_grad, loss.reshape(())

time: 49.9 us -> 47.9 us (0.960)
  local copies, waits for them, and re-layouts: 6.96 us -> 4.59 us
    unnamed x12 -> x2, local copies, waits for them, and re-layouts: 6.96 us -> 4.59 us
where the time goes in v2:
time: 47.9 us; the launch traced here: 47.6 us
  Pallas kernels  40 us (84%)
  local copies, waits for them, and re-layouts  4.59 us (10%)
  between operations  3.04 us (6%)
    pallas_call x1, Pallas kernels, on_device(): pl.pallas_call(functools.partial(kernel, n_proto, n_sample), out_shape=(j...  40 us
    unnamed x2, local copies, waits for them, and re-layouts  4.59 us

profile of v2, /device:TPU:0, one launch (start us, length us, event | category | flops | bytes accessed | tf_op | source)
XLA Modules:
  0.0 47.6 jit_solution(11400132352329449434)
XLA Ops:
  1.3 40.0 %shard_map.85 = (bf16[768,384]{1,0:T(8,128)(2,1)}, f32[1024,384]{1,0:T(8,128)}, f32[1,1]{1,0:T(1,128)}) custom-call(bf16[256,384]{1,0:T(8,128)(2,1)} %tn_hbm.1, bf16[768,384]{1,0:T(8,128)(2,1)} %q_hbm.1, bf16[256,384]{1,0:T(8,128)(2,1)} %st_hbm.1, bf16[2048,384]{1,0:T(8,128)(2,1)} %pr_hbm.1, s32[2,128]{1,0:T(2,128)} %bitcast.2, s32[1]{0:T(128)S(6)} %copy.12.head_ref), custom_call_target="tpu_custom_call" | custom-call | tf_op jit(solution)/shard_map/pallas_call | solution.py:332
  41.3 1.9 %copy.13 = bf16[768,384]{1,0:T(8,128)(2,1)} copy(bf16[768,384]{1,0:T(8,128)(2,1)} %get-tuple-element.12) | data formatting | bytes 1179648
  43.2 2.7 %copy.14 = f32[1024,384]{1,0:T(8,128)} copy(f32[1024,384]{1,0:T(8,128)} %get-tuple-element.13) | data formatting | bytes 3145728
